TPU v7x, 512 devices: a whole 4x4x16 slice. The times are simulated.
512 devices in a mesh: ctx: 32 (over z, core), inner: 16 (over y, x).
Axes of the slice: x: 4, y: 4, z: 16, core: 2. Of those that a mesh axis runs over, the one named last changes fastest.
Arguments:
- tokens: bfloat16 [65536, 2048], P(('ctx', 'inner')), may hold values from -6 to 6
- project_weight: bfloat16 [2048, 2, 4096], P('ctx', None, 'inner'), may hold values from -0.125 to 0.125
- state_weight: bfloat16 [2048, 2, 512], P('ctx', None, 'inner'), may hold values from -0.125 to 0.125
- step_weight: bfloat16 [2048, 64], P('ctx', 'inner'), may hold values from -0.125 to 0.125
- mixer_taps: float32 [5, 4096], P(None, 'inner'), may hold values from -2.5 to 2.5
- state_taps: float32 [5, 2, 512], replicated, may hold values from -2.5 to 2.5
- step_bias: float32 [64], P('inner'), may hold values from -4.6 to -2.3
- decay_log: float32 [64], P('inner'), may hold values from -13 to 0.5, as said below
- norm_gain: float32 [4096], replicated, may hold values from 0.1 to 1.9
Outputs:
- mixed_output: bfloat16 [65536, 4096], P(('ctx', 'inner'))
Inputs may be any that keep to these rules, and one draw needn't show every extreme that they name: `decay_log`: one value a head.
All inputs are finite; a program needn't handle non-finite values.
Results may differ from a plain program's by a relative error of at most 0.0075.
Values may be sent and summed in bfloat16 or wider, within the bound.
A program may use at most 64 MiB of HBM per device.

v0:
```python
import jax
import jax.numpy as jnp
from jax import lax
from jax.sharding import PartitionSpec as P

H = 64
P_SIZE = 64
N = 128
G = 4
CONV = 4
SPAN = 128
EPSILON = 1e-05


def passed_along(x, axis, by):
    count = lax.axis_size(axis)
    pairs = [(i, i + by) for i in range(count) if 0 <= i + by < count]
    return lax.ppermute(x, axis, pairs)


def entering(x, axis, join, neutral):
    place = lax.axis_index(axis)
    gathered = jax.tree.map(
        lambda a, kind: lax.all_gather(a.astype(kind), axis), x, (jnp.bfloat16, jnp.bfloat16)
    )
    state = jax.tree.map(lambda a, e: jnp.zeros_like(a) + jnp.asarray(e, a.dtype), x, neutral)

    def one(turn, state):
        return join(
            state,
            jax.tree.map(
                lambda a, own: lax.dynamic_index_in_dim(a, turn, 0, False).astype(own.dtype),
                gathered,
                x,
            ),
        )

    return lax.fori_loop(0, place, one, state)


def partner(value, axis, stride):
    mask = 2**stride
    pairs = [(source, source ^ mask) for source in range(lax.axis_size(axis))]
    return lax.ppermute(value, axis, pairs)


def conv_apply(taps, previous, current):
    extended = jnp.concatenate([previous, current], axis=0)
    length_rows = current.shape[0]
    mixed = jnp.broadcast_to(taps[CONV], current.shape)
    for offset in range(CONV):
        mixed = mixed + taps[offset] * extended[offset : offset + length_rows].astype(jnp.float32)
    return jax.nn.silu(mixed).astype(jnp.bfloat16)


def join_chain(earlier, later):
    return (earlier[0] + later[0], jnp.exp(later[0])[:, None, None] * earlier[1] + later[1])


def carry_block(state, inputs):
    decay_sum, added = inputs
    return (jnp.exp(decay_sum)[:, None, None] * state + added, state)


def pick_group(values, group):
    shaped = values.reshape(values.shape[:-1] + (N, G))
    return lax.dynamic_index_in_dim(shaped, group, shaped.ndim - 1, keepdims=False)


def on_device(
    tokens,
    project_weight,
    state_weight,
    step_weight,
    mixer_taps,
    state_taps,
    step_bias,
    decay_log,
    norm_gain,
):
    inner_id = lax.axis_index("inner")
    project_rows, state_rows, step_rows = (
        lax.all_gather(project_weight, "ctx", axis=0, tiled=True),
        lax.all_gather(state_weight, "ctx", axis=0, tiled=True),
        lax.all_gather(step_weight, "ctx", axis=0, tiled=True),
    )
    heads_here = step_weight.shape[1]
    width_here = project_weight.shape[2]
    model_width = project_rows.shape[0]
    group = inner_id * heads_here // (H // G)
    full_cols = lax.all_gather(state_rows, "inner", axis=2, tiled=True)
    slice_cols = N
    state_cols = pick_group(full_cols, group)
    state_conv = pick_group(state_taps, group)
    joined = jnp.concatenate(
        [
            project_rows.reshape(model_width, 2 * width_here),
            state_cols.reshape(model_width, 2 * slice_cols),
            step_rows,
        ],
        axis=1,
    )
    projected = jnp.dot(
        lax.all_gather(tokens, "inner", axis=0, tiled=True),
        joined,
        preferred_element_type=jnp.float32,
    ).astype(jnp.bfloat16)
    rows_total = projected.shape[0]
    gate_values = projected[:, :width_here]
    x_pre = projected[:, width_here : 2 * width_here]
    state_pre = projected[:, 2 * width_here : 2 * width_here + 2 * slice_cols].reshape(
        rows_total, 2, slice_cols
    )
    step_raw = projected[:, 2 * width_here + 2 * slice_cols :]
    edge_row = rows_total - (CONV - 1)
    prior_x, prior_state = passed_along((x_pre[edge_row:], state_pre[edge_row:]), "ctx", 1)
    x_vals = conv_apply(mixer_taps, prior_x, x_pre)
    state_vals = conv_apply(state_conv, prior_state, state_pre)
    blocks = rows_total // SPAN
    b_blocks = state_vals[:, 0].reshape(blocks, SPAN, N)
    c_blocks = state_vals[:, 1].reshape(blocks, SPAN, N)
    step_size = jax.nn.softplus(step_raw.astype(jnp.float32) + step_bias)
    step_heads = step_size.T.reshape(heads_here, blocks, SPAN)
    cumul = jnp.cumsum(step_heads * (-jnp.exp(decay_log))[:, None, None], axis=2)
    scores = jnp.einsum("ctn,csn->cts", c_blocks, b_blocks, preferred_element_type=jnp.float32)
    lower = jnp.tril(jnp.ones((SPAN, SPAN), dtype=bool))
    spacing = jnp.where(lower, cumul[..., :, None] - cumul[..., None, :], -jnp.inf)
    mixing = (scores[None] * jnp.exp(spacing) * step_heads[:, :, None, :]).astype(jnp.bfloat16)
    x_blocks = x_vals.reshape(blocks, SPAN, heads_here, P_SIZE)
    diagonal = jnp.einsum("hcts,cshp->cthp", mixing, x_blocks, preferred_element_type=jnp.float32)
    ending = cumul[:, :, -1]
    to_end = jnp.exp(ending[..., None] - cumul) * step_heads
    weighted_b = (b_blocks.astype(jnp.float32)[None] * to_end[..., None]).astype(jnp.bfloat16)
    fresh = jnp.einsum("hcsn,cshp->chnp", weighted_b, x_blocks, preferred_element_type=jnp.float32)
    empty_state = jnp.zeros((heads_here, N, P_SIZE), jnp.float32)
    block_state, local_in = lax.scan(carry_block, empty_state, (ending.T, fresh))
    block_log = jnp.sum(ending, axis=1)
    before_log = (jnp.cumsum(ending, axis=1) - ending).T
    _, prior_block = entering(
        (block_log, block_state), "ctx", join_chain, (jnp.zeros_like(block_log), empty_state)
    )
    state_in = local_in + jnp.exp(before_log)[:, :, None, None] * prior_block[None]
    c_scaled = (c_blocks.astype(jnp.float32)[None] * jnp.exp(cumul)[..., None]).astype(jnp.bfloat16)
    state_high = state_in.astype(jnp.bfloat16)
    state_low = (state_in - state_high.astype(jnp.float32)).astype(jnp.bfloat16)
    offdiag = jnp.einsum(
        "hctn,chnp->cthp", c_scaled, state_high, preferred_element_type=jnp.float32
    )
    offdiag = offdiag + jnp.einsum(
        "hctn,chnp->cthp", c_scaled, state_low, preferred_element_type=jnp.float32
    )
    outputs = (diagonal + offdiag).reshape(rows_total, width_here)
    gated = (outputs * jax.nn.silu(gate_values.astype(jnp.float32))).astype(jnp.bfloat16)
    gated_wide = gated.astype(jnp.float32)
    squares = jnp.sum(gated_wide * gated_wide, axis=1)
    group_devices = H // G // heads_here
    for bit in range(group_devices.bit_length() - 1):
        squares = squares + partner(squares, "inner", bit)
    power = squares[:, None] / (H * P_SIZE // G)
    gain_here = lax.dynamic_slice_in_dim(norm_gain, inner_id * width_here, width_here, 0)
    normed = (gated_wide * lax.rsqrt(power + EPSILON) * gain_here).astype(jnp.bfloat16)
    result = lax.all_to_all(normed, "inner", split_axis=0, concat_axis=1, tiled=True)
    return result


def solution(mesh):
    placed = (
        P(("ctx", "inner"), None),
        P("ctx", None, "inner"),
        P("ctx", None, "inner"),
        P("ctx", "inner"),
        P(None, "inner"),
        P(),
        P("inner"),
        P("inner"),
        P(),
    )
    return jax.shard_map(
        on_device, mesh=mesh, in_specs=placed, out_specs=P(("ctx", "inner"), None), check_vma=False
    )
```

profile of v0, /device:TPU:480, one launch (start us, length us, event | category | flops | bytes accessed | tf_op | source)
XLA Modules:
  0.0 455.8 jit_solution(17512234280697024061)
XLA Ops:
  8.1 30.7 %all_gather.26 = bf16[2048,2,32]{2,1,0:T(2,128)(2,1)S(1)} all-gather(bf16[64,2,32]{2,1,0:T(2,128)(2,1)S(1)} %copy.91), channel_id=1, replica_groups=mesh['ctx'=32,'inner'=16] {'ctx'}, dimensions={0}, use_global_device_ids=true | all-gather | bytes 270336 | tf_op jit(solution)/shard_map/all_gather | solution.py:84
  38.8 1.8 copy.92
  41.4 29.1 %all-gather.2 = bf16[32,64,4]{1,2,0:T(4,128)(2,1)S(1)} all-gather(bf16[1,64,4]{1,2,0:T(4,128)(2,1)S(1)} %bitcast.102), channel_id=1, replica_groups=mesh['ctx'=32,'inner'=16] {'ctx'}, dimensions={0}, use_global_device_ids=true | all-gather | bytes 16896 | tf_op jit(solution)/shard_map/all_gather | solution.py:85
  72.8 6.1 %all-gather.8.cloned.1.call-done = bf16[2048,2,256]{2,1,0:T(2,128)(2,1)} async-done(((bf16[64,2,256]{2,1,0:T(2,128)(2,1)}), bf16[2048,2,256]{2,1,0:T(2,128)(2,1)}) %all-gather.8.cloned.1.call-update) | async-done | bytes 2097168 | tf_op jit(solution)/shard_map/all_gather | solution.py:83
  78.9 2.0 copy.123
  81.0 66.3 %all-gather.10.cloned.1.call-done = bf16[2048,2,512]{0,1,2:T(2,128)(2,1)} async-done(((bf16[2048,2,32]{0,1,2:T(2,128)(2,1)}), bf16[2048,2,512]{0,1,2:T(2,128)(2,1)}) %all-gather.10.cloned.1.call-update) | async-done | bytes 4194320 | tf_op jit(solution)/shard_map/all_gather | solution.py:91
  147.3 1.9 constant_dynamic-slice_fusion.2
  149.6 1.3 copy.95
  150.9 85.3 %all-gather.12.cloned.1.call-done = bf16[2048,2048]{1,0:T(8,128)(2,1)} async-done(((bf16[128,2048]{1,0:T(8,128)(2,1)}), bf16[2048,2048]{1,0:T(8,128)(2,1)}) %all-gather.12.cloned.1.call-update) | async-done | bytes 8388624 | tf_op jit(solution)/shard_map/all_gather | solution.py:104
  236.1 10.8 %fusion.12 = bf16[2048,772]{0,1:T(8,128)(2,1)S(1)} fusion(bf16[2048,2048]{1,0:T(8,128)(2,1)} %all-gather.12.cloned.1.call-done, bf16[2048,4]{1,0:T(8,128)(2,1)} %bitcast.92, bf16[2048,256]{1,0:T(8,128)(2,1)} %copy.95, bf16[2048,512]{1,0:T(8,128)(2,1)S(1)} %bitcast.91), kind=kOutput, calls=%fused_computation.21 | convolution fusion | flops 6487072768 | bytes 14712832 | tf_op jit(solution)/shard_map/dot_general | solution.py:103
  247.2 1.4 copy-done.1
  250.2 1.9 collective-permute-start
  252.2 2.1 collective-permute-start.1
  254.4 1.4 collective-permute-done
  255.7 2.2 fusion.51
  258.2 2.2 multiply_convert_fusion.7
  260.8 3.9 fusion.26
  264.7 28.8 %while.26 = (s32[]{:T(128)}, f32[4,128,64]{2,1,0:T(8,128)S(1)}, f32[16,4,128,64]{3,2,1,0:T(8,128)}, f32[16,4]{1,0:T(8,128)S(1)}, f32[16,4,128,64]{3,2,1,0:T(8,128)}, /*index=5*/s32[]{:T(128)}, s32[]{:T(128)}) while((s32[]{:T(128)}, f32[4,128,64]{2,1,0:T(8,128)S(1)}, f32[16,4,128,64]{3,2,1,0:T(8,128)}, f32[16,4]{1,0:T(8,128)S(1)}, ...), condition=%wide.region_2.3_spmd.clone, body=%wide.region_1.2_spmd.clone.sunk | while | flops 131075 | bytes 787088 | solution.py:136
  294.4 1.3 dynamic-slice
  296.8 42.4 %all-reduce = bf16[128]{0:T(256)(128)(2,1)S(1)} all-reduce(bf16[128]{0:T(256)(128)(2,1)S(1)} %dynamic-update-slice), channel_id=2, replica_groups=mesh['ctx'=32,'inner'=16] {'ctx'}, use_global_device_ids=true, to_apply=%add | all-reduce | flops 128 | bytes 512
  340.3 3.3 fusion.18
  343.6 22.2 %all-gather.14.cloned.1.call-done = bf16[128,128,64]{1,2,0:T(8,128)(2,1)} async-done(((bf16[4,128,64]{1,2,0:T(8,128)(2,1)}), bf16[128,128,64]{1,2,0:T(8,128)(2,1)}) %all-gather.14.cloned.1.call-update) | async-done | bytes 2097168 | tf_op jit(solution)/shard_map/all_gather | solution.py:24
  365.8 34.4 %while.25 = (s32[]{:T(128)}, f32[4,128,64]{2,1,0:T(8,128)S(1)}, s32[]{:T(128)}, bf16[32,4]{1,0:T(8,128)(2,1)S(1)}, bf16[32,4,128,64]{2,3,1,0:T(8,128)(2,1)}, /*index=5*/s32[]{:T(128)}, s32[]{:T(128)}, s32[]{:T(128)}) while((s32[]{:T(128)}, f32[4,128,64]{2,1,0:T(8,128)S(1)}, s32[]{:T(128)}, bf16[32,4]{1,0:T(8,128)(2,1)S(1)}, ...), condition=%wide.region_6.7_spmd, body=%wide.region_5.6_spmd.sunk | while | flops 98313 | bytes 589991 | solution.py:38
  400.2 5.2 %fusion.15 = f32[16,4,64,128]{3,2,1,0:T(8,128)S(1)} fusion(f32[16,4,128,64]{3,2,1,0:T(8,128)} %get-tuple-element.77, f32[4,16,128]{2,0,1:T(4,128)S(1)} %copy.110, f32[16,128,128]{2,1,0:T(8,128)S(1)} %convert_element_type.135, f32[4,128,64]{2,1,0:T(8,128)S(1)} %get-tuple-element.79, f32[16,4]{1,0:T(8,128)S(1)} %copy.107), kind=kOutput, calls=%fused_computation.22 | convolution fusion | flops 139460608 | bytes 5406976 | tf_op jit(solution)/shard_map/hctn,chnp->cthp/dot_general | solution.py:149
  405.5 2.7 add_bitcast_fusion
  409.4 2.4 fusion.23
  411.8 3.4 collective-permute-start.2
  415.2 2.2 collective-permute-done.2
  417.4 4.9 %collective-permute-start.3 = (f32[2048]{0:T(1024)S(1)}, f32[2048]{0:T(1024)S(1)}, u32[]{:S(2)}, u32[]{:S(2)}) collective-permute-start(f32[2048]{0:T(1024)S(1)} %add.124), channel_id=1, source_target_pairs={{0,2},{1,3},{2,0},{3,1},{4,6},{5,7},{6,4},{7,5},{8,10},{9,11},{10,... | collective-permute-start | bytes 24584 | tf_op jit(solution)/shard_map/ppermute | solution.py:44
  423.0 1.4 collective-permute-done.3
  424.8 23.1 %all_to_all.19 = bf16[16,128,256]{1,2,0:T(8,128)(2,1)S(1)} all-to-all(bf16[16,128,256]{1,2,0:T(8,128)(2,1)S(1)} %copy_bitcast_fusion), channel_id=1, replica_groups=mesh['ctx'=32,'inner'=16] {'inner'}, dimensions={0} | all-to-all | bytes 2097152 | tf_op jit(solution)/shard_map/all_to_all | solution.py:162
  448.0 1.3 copy.115
  (233 shorter events, 73.9 us)
Async XLA Ops:
  6.5 34.9 %copy-start.5 = (bf16[64,4]{0,1:T(4,128)(2,1)S(1)}, bf16[64,4]{0,1:T(4,128)(2,1)}, u32[]{:S(2)}) copy-start(bf16[64,4]{0,1:T(4,128)(2,1)} %param.16) | copy-start | bytes 1540
  6.5 65.1 %copy-start.3 = (f32[5,2,512]{2,1,0:T(2,128)S(1)}, f32[5,2,512]{2,1,0:T(2,128)}, u32[]{:S(2)}) copy-start(f32[5,2,512]{2,1,0:T(2,128)} %param.18) | copy-start | bytes 61444
  6.5 72.4 %all-gather.8.cloned.1.call-start = ((), (), s32[]{:S(2)}) async-start(), calls=%async_computation.1 | async-start | bytes 2162688 | tf_op jit(solution)/shard_map/all_gather | solution.py:83
  7.3 140.0 %all-gather.10.cloned.1.call-start = ((), (), s32[]{:S(2)}) async-start(), calls=%async_computation.2 | async-start | bytes 4456448 | tf_op jit(solution)/shard_map/all_gather | solution.py:91
  38.8 34.0 %copy-start.7 = (f32[4]{0:T(128)S(1)}, f32[4]{0:T(128)}, u32[]{:S(2)}) copy-start(f32[4]{0:T(128)} %param.20) | copy-start | bytes 52
  38.8 34.0 %copy-start.4 = (f32[5,256]{1,0:T(8,128)S(1)}, f32[5,256]{1,0:T(8,128)}, u32[]{:S(2)}) copy-start(f32[5,256]{1,0:T(8,128)} %param.17) | copy-start | bytes 15364
  40.6 195.5 %all-gather.12.cloned.1.call-start = ((), (), s32[]{:S(2)}) async-start(), calls=%async_computation.3 | async-start | bytes 8912896 | tf_op jit(solution)/shard_map/all_gather | solution.py:104
  41.3 324.5 %all-gather.14.cloned.1.call-start = ((), (), s32[]{:S(2)}) async-start(), calls=%async_computation.4 | async-start | bytes 2162688 | tf_op jit(solution)/shard_map/all_gather | solution.py:24
  246.9 1.7 copy-start.1
  247.0 1.7 copy-start.6
  250.2 5.6 %collective-permute-start = (bf16[3,256]{0,1:T(8,128)(2,1)S(1)}, bf16[3,256]{0,1:T(8,128)(2,1)S(1)}, u32[]{:S(2)}, u32[]{:S(2)}) collective-permute-start(bf16[3,256]{0,1:T(8,128)(2,1)S(1)} %get-tuple-element.164), channel_id=1, source_target_pairs={{0,16},{16,32},{32,48},{48,64},{64,80},{80,96},{96,112},{112,128},... | collective-permute-start | bytes 4616 | tf_op jit(solution)/shard_map/ppermute | solution.py:18
  252.2 5.9 %collective-permute-start.1 = (bf16[3,2,128]{0,2,1:T(8,128)(2,1)S(1)}, bf16[3,2,128]{0,2,1:T(8,128)(2,1)S(1)}, u32[]{:S(2)}, u32[]{:S(2)}) collective-permute-start(bf16[3,2,128]{0,2,1:T(8,128)(2,1)S(1)} %bitcast.94), channel_id=1, source_target_pairs={{0,16},{16,32},{32,48},{48,64},{64,80},{80,96},{96,112},{112,128},... | collective-permute-start | bytes 4616 | tf_op jit(solution)/shard_map/ppermute | solution.py:18
  400.2 5.2 %copy-start = (f32[16,4,128,64]{3,2,1,0:T(8,128)S(1)}, f32[16,4,128,64]{3,2,1,0:T(8,128)}, u32[]{:S(2)}) copy-start(f32[16,4,128,64]{3,2,1,0:T(8,128)} %get-tuple-element.77) | copy-start | bytes 6291460
  400.2 5.2 %copy-start.2 = (f32[16,4,64,128]{3,2,1,0:T(8,128)S(1)}, f32[16,4,64,128]{3,2,1,0:T(8,128)}, u32[]{:S(2)}) copy-start(f32[16,4,64,128]{3,2,1,0:T(8,128)} %fusion.18) | copy-start | bytes 6291460
  411.8 5.5 %collective-permute-start.2 = (f32[2048]{0:T(1024)S(1)}, f32[2048]{0:T(1024)S(1)}, u32[]{:S(2)}, u32[]{:S(2)}) collective-permute-start(f32[2048]{0:T(1024)S(1)} %get-tuple-element.160), channel_id=1, source_target_pairs={{0,1},{1,0},{2,3},{3,2},{4,5},{5,4},{6,7},{7,6},{8,9},{9,8},{10,11... | collective-permute-start | bytes 24584 | tf_op jit(solution)/shard_map/ppermute | solution.py:44
  417.4 7.0 %collective-permute-start.3 = (f32[2048]{0:T(1024)S(1)}, f32[2048]{0:T(1024)S(1)}, u32[]{:S(2)}, u32[]{:S(2)}) collective-permute-start(f32[2048]{0:T(1024)S(1)} %add.124), channel_id=1, source_target_pairs={{0,2},{1,3},{2,0},{3,1},{4,6},{5,7},{6,4},{7,5},{8,10},{9,11},{10,... | collective-permute-start | bytes 24584 | tf_op jit(solution)/shard_map/ppermute | solution.py:44
Sparse Core Ops, SparseCore 0:
  9.5 69.3 all-gather.7
  81.9 65.2 all-gather.9
  150.3 85.8 all-gather.11
  294.5 71.2 all-gather.13
where the time goes:
time: 458 us; the launch traced here: 456 us
  waiting for transfers between devices  186 us (41%)
  blocking collectives  125 us (27%)
  local copies, waits for them, and re-layouts  48.5 us (11%)
  other arithmetic  41.3 us (9%)
  matrix products  26.4 us (6%)
  between operations  14.2 us (3%)
  starting transfers between devices  12.4 us (3%)
    all_gather x1, waiting for transfers between devices, on_device(): lax.all_gather(tokens, 'inner', axis=0, tiled=True)  85.3 us
    all_gather x1, waiting for transfers between devices, on_device(): full_cols = lax.all_gather(state_rows, 'inner', axis=2, tiled=True)  66.3 us
    unnamed x1, blocking collectives  42.4 us
    all_gather x1, blocking collectives, on_device(): lax.all_gather(state_weight, 'ctx', axis=0, tiled=True)  30.7 us
    dynamic_slice x60, local copies, waits for them, and re-layouts, one(): lax.dynamic_index_in_dim(a, turn, 0, False).astype(own.dtype)  29.4 us
    all_gather x1, blocking collectives, on_device(): lax.all_gather(step_weight, 'ctx', axis=0, tiled=True)  29.1 us
    all_to_all x1, blocking collectives, on_device(): lax.all_to_all(normed, 'inner', split_axis=0, concat_axis=1, tiled=True)  23.1 us
    all_gather x1, waiting for transfers between devices, entering(): lax.all_gather(a.astype(kind), axis)  22.2 us
  transfers between devices with their start and end apart: 8, of which 7 were waited for; matrix products, arithmetic and copies ran while one was open for 4% of the time, Pallas kernels for 0%

commit v1 on v0

--- a/solution.py
+++ b/solution.py
@@ -88,7 +88,14 @@
     width_here = project_weight.shape[2]
     model_width = project_rows.shape[0]
     group = inner_id * heads_here // (H // G)
-    full_cols = lax.all_gather(state_rows, "inner", axis=2, tiled=True)
+    devices = lax.axis_size("inner")
+    right = [(i_2, (i_2 + 1) % devices) for i_2 in range(devices)]
+    pieces = [state_rows]
+    for hop in range(1, devices):
+        pieces = [lax.ppermute(pieces[0], "inner", right), *pieces]
+    result_2 = jnp.concatenate(pieces, axis=2)
+    shift = (lax.axis_index("inner") + 1) * pieces[-1].shape[2]
+    full_cols = jnp.roll(result_2, shift, axis=2)
     slice_cols = N
     state_cols = pick_group(full_cols, group)
     state_conv = pick_group(state_taps, group)

time: 458 us -> 719 us (1.57)
  local copies, waits for them, and re-layouts: 48.5 us -> 264 us
  starting transfers between devices: 12.4 us -> 43.3 us
    ppermute x0 -> x15, waiting for transfers between devices: none -> 165 us  [on_device(): pieces = [lax.ppermute(pieces[0], 'inner', right), *pieces]]
    concatenate x0 -> x1, local copies, waits for them, and re-layouts: none -> 135 us  [on_device(): full_cols = jnp.roll(result_2, shift, axis=2)]
    all_gather x1, waiting for transfers between devices: 85.3 us -> 0.02 us  [on_device(): lax.all_gather(tokens, 'inner', axis=0, tiled=True)]
    all_gather x1 -> x0, waiting for transfers between devices: 66.3 us -> none  [on_device(): full_cols = lax.all_gather(state_rows, 'inner', axis=2, tiled=True)]
    ppermute x0 -> x15, local copies, waits for them, and re-layouts: none -> 47.5 us  [on_device(): pieces = [lax.ppermute(pieces[0], 'inner', right), *pieces]]
    ppermute x0 -> x15, starting transfers between devices: none -> 30.8 us  [on_device(): pieces = [lax.ppermute(pieces[0], 'inner', right), *pieces]]
    dynamic_slice x0 -> x2, local copies, waits for them, and re-layouts: none -> 26.9 us  [on_device(): full_cols = jnp.roll(result_2, shift, axis=2)]
  transfers between devices with their start and end apart: 8 -> 22, of which waited for: 7 -> 18; matrix products, arithmetic and copies ran while one was open for 4% -> 32% of each run, Pallas kernels for 0% -> 0%
where the time goes in v1:
time: 719 us; the launch traced here: 711 us
  local copies, waits for them, and re-layouts  264 us (37%)
  waiting for transfers between devices  192 us (27%)
  blocking collectives  126 us (18%)
  starting transfers between devices  43.3 us (6%)
  other arithmetic  42.9 us (6%)
  matrix products  26.1 us (4%)
  between operations  14.5 us (2%)
    ppermute x15, waiting for transfers between devices, on_device(): pieces = [lax.ppermute(pieces[0], 'inner', right), *pieces]  165 us
    concatenate x1, local copies, waits for them, and re-layouts, on_device(): full_cols = jnp.roll(result_2, shift, axis=2)  135 us
    ppermute x15, local copies, waits for them, and re-layouts, on_device(): pieces = [lax.ppermute(pieces[0], 'inner', right), *pieces]  47.5 us
    unnamed x1, blocking collectives  44 us
    ppermute x15, starting transfers between devices, on_device(): pieces = [lax.ppermute(pieces[0], 'inner', right), *pieces]  30.8 us
    all_gather x1, blocking collectives, on_device(): lax.all_gather(state_weight, 'ctx', axis=0, tiled=True)  30 us
    all_gather x1, blocking collectives, on_device(): lax.all_gather(step_weight, 'ctx', axis=0, tiled=True)  29.4 us
    dynamic_slice x60, local copies, waits for them, and re-layouts, one(): lax.dynamic_index_in_dim(a, turn, 0, False).astype(own.dtype)  29.4 us
  transfers between devices with their start and end apart: 22, of which 18 were waited for; matrix products, arithmetic and copies ran while one was open for 32% of the time, Pallas kernels for 0%

profile of v1, /device:TPU:480, one launch (start us, length us, event | category | flops | bytes accessed | tf_op | source)
XLA Modules:
  0.0 710.8 jit_solution(13747331429049006565)
XLA Ops:
  8.9 30.0 %all_gather.23 = bf16[2048,2,32]{2,1,0:T(2,128)(2,1)S(1)} all-gather(bf16[64,2,32]{2,1,0:T(2,128)(2,1)S(1)} %copy.116), channel_id=1, replica_groups=mesh['ctx'=32,'inner'=16] {'ctx'}, dimensions={0}, use_global_device_ids=true | all-gather | bytes 270336 | tf_op jit(solution)/shard_map/all_gather | solution.py:84
  39.5 4.1 collective-permute-start
  43.6 10.7 %collective-permute-done = bf16[2048,2,32]{0,2,1:T(8,128)(2,1)S(1)} collective-permute-done((bf16[2048,2,32]{0,2,1:T(8,128)(2,1)S(1)}, bf16[2048,2,32]{0,2,1:T(8,128)(2,1)S(1)}, u32[]{:S(2)}, u32[]{:S(2)}) %collective-permute-start) | collective-permute-done | bytes 262176 | tf_op jit(solution)/shard_map/ppermute | solution.py:95
  56.3 11.3 %collective-permute-done.1 = bf16[2048,2,32]{0,2,1:T(8,128)(2,1)S(1)} collective-permute-done((bf16[2048,2,32]{0,2,1:T(8,128)(2,1)S(1)}, bf16[2048,2,32]{0,2,1:T(8,128)(2,1)S(1)}, u32[]{:S(2)}, u32[]{:S(2)}) %collective-permute-start.1) | collective-permute-done | bytes 262176 | tf_op jit(solution)/shard_map/ppermute | solution.py:95
  69.5 10.4 %collective-permute-done.2 = bf16[2048,2,32]{0,2,1:T(8,128)(2,1)S(1)} collective-permute-done((bf16[2048,2,32]{0,2,1:T(8,128)(2,1)S(1)}, bf16[2048,2,32]{0,2,1:T(8,128)(2,1)S(1)}, u32[]{:S(2)}, u32[]{:S(2)}) %collective-permute-start.2) | collective-permute-done | bytes 262176 | tf_op jit(solution)/shard_map/ppermute | solution.py:95
  81.8 9.7 %collective-permute-done.3 = bf16[2048,2,32]{0,2,1:T(8,128)(2,1)S(1)} collective-permute-done((bf16[2048,2,32]{0,2,1:T(8,128)(2,1)S(1)}, bf16[2048,2,32]{0,2,1:T(8,128)(2,1)S(1)}, u32[]{:S(2)}, u32[]{:S(2)}) %collective-permute-start.3) | collective-permute-done | bytes 262176 | tf_op jit(solution)/shard_map/ppermute | solution.py:95
  93.3 9.7 %collective-permute-done.4 = bf16[2048,2,32]{0,2,1:T(8,128)(2,1)S(1)} collective-permute-done((bf16[2048,2,32]{0,2,1:T(8,128)(2,1)S(1)}, bf16[2048,2,32]{0,2,1:T(8,128)(2,1)S(1)}, u32[]{:S(2)}, u32[]{:S(2)}) %collective-permute-start.4) | collective-permute-done | bytes 262176 | tf_op jit(solution)/shard_map/ppermute | solution.py:95
  105.0 13.2 %collective-permute-done.5 = bf16[2048,2,32]{0,2,1:T(8,128)(2,1)S(1)} collective-permute-done((bf16[2048,2,32]{0,2,1:T(8,128)(2,1)S(1)}, bf16[2048,2,32]{0,2,1:T(8,128)(2,1)S(1)}, u32[]{:S(2)}, u32[]{:S(2)}) %collective-permute-start.5) | collective-permute-done | bytes 262176 | tf_op jit(solution)/shard_map/ppermute | solution.py:95
  120.8 9.7 %collective-permute-done.6 = bf16[2048,2,32]{0,2,1:T(8,128)(2,1)S(1)} collective-permute-done((bf16[2048,2,32]{0,2,1:T(8,128)(2,1)S(1)}, bf16[2048,2,32]{0,2,1:T(8,128)(2,1)S(1)}, u32[]{:S(2)}, u32[]{:S(2)}) %collective-permute-start.6) | collective-permute-done | bytes 262176 | tf_op jit(solution)/shard_map/ppermute | solution.py:95
  133.1 15.9 %collective-permute-done.7 = bf16[2048,2,32]{0,2,1:T(8,128)(2,1)S(1)} collective-permute-done((bf16[2048,2,32]{0,2,1:T(8,128)(2,1)S(1)}, bf16[2048,2,32]{0,2,1:T(8,128)(2,1)S(1)}, u32[]{:S(2)}, u32[]{:S(2)}) %collective-permute-start.7) | collective-permute-done | bytes 262176 | tf_op jit(solution)/shard_map/ppermute | solution.py:95
  151.6 15.6 %collective-permute-done.8 = bf16[2048,2,32]{0,2,1:T(8,128)(2,1)S(1)} collective-permute-done((bf16[2048,2,32]{0,2,1:T(8,128)(2,1)S(1)}, bf16[2048,2,32]{0,2,1:T(8,128)(2,1)S(1)}, u32[]{:S(2)}, u32[]{:S(2)}) %collective-permute-start.8) | collective-permute-done | bytes 262176 | tf_op jit(solution)/shard_map/ppermute | solution.py:95
  169.7 15.3 %collective-permute-done.9 = bf16[2048,2,32]{0,2,1:T(8,128)(2,1)S(1)} collective-permute-done((bf16[2048,2,32]{0,2,1:T(8,128)(2,1)S(1)}, bf16[2048,2,32]{0,2,1:T(8,128)(2,1)S(1)}, u32[]{:S(2)}, u32[]{:S(2)}) %collective-permute-start.9) | collective-permute-done | bytes 262176 | tf_op jit(solution)/shard_map/ppermute | solution.py:95
  187.7 9.7 %collective-permute-done.10 = bf16[2048,2,32]{0,2,1:T(8,128)(2,1)S(1)} collective-permute-done((bf16[2048,2,32]{0,2,1:T(8,128)(2,1)S(1)}, bf16[2048,2,32]{0,2,1:T(8,128)(2,1)S(1)}, u32[]{:S(2)}, u32[]{:S(2)}) %collective-permute-start.10) | collective-permute-done | bytes 262176 | tf_op jit(solution)/shard_map/ppermute | solution.py:95
  199.9 10.7 %collective-permute-done.11 = bf16[2048,2,32]{0,2,1:T(8,128)(2,1)S(1)} collective-permute-done((bf16[2048,2,32]{0,2,1:T(8,128)(2,1)S(1)}, bf16[2048,2,32]{0,2,1:T(8,128)(2,1)S(1)}, u32[]{:S(2)}, u32[]{:S(2)}) %collective-permute-start.11) | collective-permute-done | bytes 262176 | tf_op jit(solution)/shard_map/ppermute | solution.py:95
  213.3 12.0 %collective-permute-done.12 = bf16[2048,2,32]{0,2,1:T(8,128)(2,1)S(1)} collective-permute-done((bf16[2048,2,32]{0,2,1:T(8,128)(2,1)S(1)}, bf16[2048,2,32]{0,2,1:T(8,128)(2,1)S(1)}, u32[]{:S(2)}, u32[]{:S(2)}) %collective-permute-start.12) | collective-permute-done | bytes 262176 | tf_op jit(solution)/shard_map/ppermute | solution.py:95
  227.9 11.6 %collective-permute-done.13 = bf16[2048,2,32]{0,2,1:T(8,128)(2,1)} collective-permute-done((bf16[2048,2,32]{0,2,1:T(8,128)(2,1)S(1)}, bf16[2048,2,32]{0,2,1:T(8,128)(2,1)}, u32[]{:S(2)}, u32[]{:S(2)}) %collective-permute-start.13) | collective-permute-done | bytes 262176 | tf_op jit(solution)/shard_map/ppermute | solution.py:95
  241.4 29.4 %all-gather.2 = bf16[32,64,4]{1,2,0:T(4,128)(2,1)S(1)} all-gather(bf16[1,64,4]{1,2,0:T(4,128)(2,1)S(1)} %bitcast.101), channel_id=1, replica_groups=mesh['ctx'=32,'inner'=16] {'ctx'}, dimensions={0}, use_global_device_ids=true | all-gather | bytes 16896 | tf_op jit(solution)/shard_map/all_gather | solution.py:85
  276.7 3.5 copy.130
  280.1 3.4 copy.129
  297.3 3.5 copy.124
  321.2 134.7 %concatenate.15 = bf16[2048,2,1024]{2,1,0:T(2,128)(2,1)} concatenate(bf16[2048,2,32]{2,1,0:T(2,128)(2,1)} %copy.118, bf16[2048,2,32]{2,1,0:T(2,128)(2,1)} %copy.119, bf16[2048,2,32]{2,1,0:T(2,128)(2,1)} %copy.120, bf16[2048,2,32]{2,1,0:T(2,128)(2,1)} %copy.121, bf16[2048,2,32]{2,1,0:T(2,128)(2,1)} %copy.122, bf16[2048,2,32]{2,1,0:T(2,128)(2,1)} %copy.123, ...), dimensions={2} | concatenate | bytes 16777216 | tf_op jit(solution)/shard_map/jit(_roll_dynamic)/concatenate | solution.py:98
  456.0 11.0 %constant_dynamic-slice_fusion.3 = bf16[2048,2,512]{2,1,0:T(2,128)(2,1)} fusion(bf16[2048,2,1024]{2,1,0:T(2,128)(2,1)} %concatenate.15, s32[]{:T(128)S(6)} %select_n.44), kind=kLoop, calls=%fused_computation.86 | loop fusion | bytes 8388612 | tf_op jit(solution)/shard_map/jit(_roll_dynamic)/dynamic_slice | solution.py:98
  466.9 15.9 %copy.148 = bf16[2048,2,512]{0,1,2:T(2,128)(2,1)} copy(bf16[2048,2,512]{2,1,0:T(2,128)(2,1)} %constant_dynamic-slice_fusion.3) | data formatting | bytes 8388608 | tf_op jit(solution)/shard_map/jit(_roll_dynamic)/dynamic_slice | solution.py:98
  487.8 10.4 %fusion.12 = bf16[2048,772]{0,1:T(8,128)(2,1)S(1)} fusion(bf16[2048,2048]{1,0:T(8,128)(2,1)} %all-gather.9.cloned.1.call-done, bf16[2048,4]{1,0:T(8,128)(2,1)} %bitcast.93, bf16[2048,256]{1,0:T(8,128)(2,1)S(1)} %copy.151, bf16[2048,512]{1,0:T(8,128)(2,1)S(1)} %bitcast.92), kind=kOutput, calls=%fused_computation.21 | convolution fusion | flops 6487072768 | bytes 14712832 | tf_op jit(solution)/shard_map/dot_general | solution.py:110
  515.3 4.0 fusion.26
  519.3 28.7 %while.26 = (s32[]{:T(128)}, f32[4,128,64]{2,1,0:T(8,128)S(1)}, f32[16,4,128,64]{3,2,1,0:T(8,128)}, f32[16,4]{1,0:T(8,128)S(1)}, f32[16,4,128,64]{3,2,1,0:T(8,128)}, /*index=5*/s32[]{:T(128)}, s32[]{:T(128)}) while((s32[]{:T(128)}, f32[4,128,64]{2,1,0:T(8,128)S(1)}, f32[16,4,128,64]{3,2,1,0:T(8,128)}, f32[16,4]{1,0:T(8,128)S(1)}, ...), condition=%wide.region_2.3_spmd.clone, body=%wide.region_1.2_spmd.clone.sunk | while | flops 131075 | bytes 787088 | solution.py:143
  551.4 44.0 %all-reduce = bf16[128]{0:T(256)(128)(2,1)S(1)} all-reduce(bf16[128]{0:T(256)(128)(2,1)S(1)} %dynamic-update-slice), channel_id=2, replica_groups=mesh['ctx'=32,'inner'=16] {'ctx'}, use_global_device_ids=true, to_apply=%add | all-reduce | flops 128 | bytes 512
  600.5 20.4 %all-gather.11.cloned.1.call-done = bf16[128,128,64]{1,2,0:T(8,128)(2,1)} async-done(((bf16[4,128,64]{1,2,0:T(8,128)(2,1)}), bf16[128,128,64]{1,2,0:T(8,128)(2,1)}) %all-gather.11.cloned.1.call-update) | async-done | bytes 2097168 | tf_op jit(solution)/shard_map/all_gather | solution.py:24
  621.0 34.3 %while.25 = (s32[]{:T(128)}, f32[4,128,64]{2,1,0:T(8,128)S(1)}, s32[]{:T(128)}, bf16[32,4]{1,0:T(8,128)(2,1)S(1)}, bf16[32,4,128,64]{2,3,1,0:T(8,128)(2,1)}, /*index=5*/s32[]{:T(128)}, s32[]{:T(128)}, s32[]{:T(128)}) while((s32[]{:T(128)}, f32[4,128,64]{2,1,0:T(8,128)S(1)}, s32[]{:T(128)}, bf16[32,4]{1,0:T(8,128)(2,1)S(1)}, ...), condition=%wide.region_6.7_spmd, body=%wide.region_5.6_spmd.sunk | while | flops 98313 | bytes 589991 | solution.py:38
  655.4 5.2 fusion.15
  672.5 4.8 collective-permute-start.18
  679.9 23.0 %all_to_all.19 = bf16[16,128,256]{1,2,0:T(8,128)(2,1)S(1)} all-to-all(bf16[16,128,256]{1,2,0:T(8,128)(2,1)S(1)} %copy_bitcast_fusion), channel_id=1, replica_groups=mesh['ctx'=32,'inner'=16] {'inner'}, dimensions={0} | all-to-all | bytes 2097152 | tf_op jit(solution)/shard_map/all_to_all | solution.py:169
  (326 shorter events, 182.2 us)
Async XLA Ops:
  6.5 234.8 %copy-start.31 = (f32[4]{0:T(128)S(1)}, f32[4]{0:T(128)}, u32[]{:S(2)}) copy-start(f32[4]{0:T(128)} %param.20) | copy-start | bytes 52
  6.5 234.9 %copy-start.28 = (bf16[64,4]{0,1:T(4,128)(2,1)S(1)}, bf16[64,4]{0,1:T(4,128)(2,1)}, u32[]{:S(2)}) copy-start(bf16[64,4]{0,1:T(4,128)(2,1)} %param.16) | copy-start | bytes 1540
  6.5 265.4 %copy-start.22 = (f32[5,2,512]{2,1,0:T(2,128)S(1)}, f32[5,2,512]{2,1,0:T(2,128)}, u32[]{:S(2)}) copy-start(f32[5,2,512]{2,1,0:T(2,128)} %param.18) | copy-start | bytes 61444
  6.5 479.2 %all-gather.7.cloned.1.call-start = ((), (), s32[]{:S(2)}) async-start(), calls=%async_computation.1 | async-start | bytes 2162688 | tf_op jit(solution)/shard_map/all_gather | solution.py:83
  7.3 480.5 %all-gather.9.cloned.1.call-start = ((), (), s32[]{:S(2)}) async-start(), calls=%async_computation.2 | async-start | bytes 8912896 | tf_op jit(solution)/shard_map/all_gather | solution.py:111
  8.0 612.9 %all-gather.11.cloned.1.call-start = ((), (), s32[]{:S(2)}) async-start(), calls=%async_computation.3 | async-start | bytes 2162688 | tf_op jit(solution)/shard_map/all_gather | solution.py:24
  8.9 264.8 %copy-start.27 = (f32[5,256]{1,0:T(8,128)S(1)}, f32[5,256]{1,0:T(8,128)}, u32[]{:S(2)}) copy-start(f32[5,256]{1,0:T(8,128)} %param.17) | copy-start | bytes 15364
  39.5 14.8 %collective-permute-start = (bf16[2048,2,32]{0,2,1:T(8,128)(2,1)S(1)}, bf16[2048,2,32]{0,2,1:T(8,128)(2,1)S(1)}, u32[]{:S(2)}, u32[]{:S(2)}) collective-permute-start(bf16[2048,2,32]{0,2,1:T(8,128)(2,1)S(1)} %copy.117), channel_id=1, source_target_pairs={{0,1},{1,2},{2,3},{3,4},{4,5},{5,6},{6,7},{7,8},{8,9},{9,10},{10,1... | collective-permute-start | bytes 786440 | tf_op jit(solution)/shard_map/ppermute | solution.py:95
  54.4 13.2 %collective-permute-start.1 = (bf16[2048,2,32]{0,2,1:T(8,128)(2,1)S(1)}, bf16[2048,2,32]{0,2,1:T(8,128)(2,1)S(1)}, u32[]{:S(2)}, u32[]{:S(2)}) collective-permute-start(bf16[2048,2,32]{0,2,1:T(8,128)(2,1)S(1)} %collective-permute-done), channel_id=1, source_target_pairs={{0,1},{1,2},{2,3},{3,4},{4,5},{5,6},{6,7},{7,8},{8,9},{9,10},{10,1... | collective-permute-start | bytes 786440 | tf_op jit(solution)/shard_map/ppermute | solution.py:95
  67.5 203.3 %copy-start.7 = (bf16[2048,2,32]{0,2,1:T(8,128)(2,1)}, bf16[2048,2,32]{0,2,1:T(8,128)(2,1)S(1)}, u32[]{:S(2)}) copy-start(bf16[2048,2,32]{0,2,1:T(8,128)(2,1)S(1)} %collective-permute-done.1) | copy-start | bytes 786436
  67.5 12.3 %collective-permute-start.2 = (bf16[2048,2,32]{0,2,1:T(8,128)(2,1)S(1)}, bf16[2048,2,32]{0,2,1:T(8,128)(2,1)S(1)}, u32[]{:S(2)}, u32[]{:S(2)}) collective-permute-start(bf16[2048,2,32]{0,2,1:T(8,128)(2,1)S(1)} %collective-permute-done.1), channel_id=1, source_target_pairs={{0,1},{1,2},{2,3},{3,4},{4,5},{5,6},{6,7},{7,8},{8,9},{9,10},{10,1... | collective-permute-start | bytes 786440 | tf_op jit(solution)/shard_map/ppermute | solution.py:95
  79.8 191.0 %copy-start.8 = (bf16[2048,2,32]{0,2,1:T(8,128)(2,1)}, bf16[2048,2,32]{0,2,1:T(8,128)(2,1)S(1)}, u32[]{:S(2)}) copy-start(bf16[2048,2,32]{0,2,1:T(8,128)(2,1)S(1)} %collective-permute-done.2) | copy-start | bytes 786436
  79.8 11.6 %collective-permute-start.3 = (bf16[2048,2,32]{0,2,1:T(8,128)(2,1)S(1)}, bf16[2048,2,32]{0,2,1:T(8,128)(2,1)S(1)}, u32[]{:S(2)}, u32[]{:S(2)}) collective-permute-start(bf16[2048,2,32]{0,2,1:T(8,128)(2,1)S(1)} %collective-permute-done.2), channel_id=1, source_target_pairs={{0,1},{1,2},{2,3},{3,4},{4,5},{5,6},{6,7},{7,8},{8,9},{9,10},{10,1... | collective-permute-start | bytes 786440 | tf_op jit(solution)/shard_map/ppermute | solution.py:95
  91.4 179.4 %copy-start.9 = (bf16[2048,2,32]{0,2,1:T(8,128)(2,1)}, bf16[2048,2,32]{0,2,1:T(8,128)(2,1)S(1)}, u32[]{:S(2)}) copy-start(bf16[2048,2,32]{0,2,1:T(8,128)(2,1)S(1)} %collective-permute-done.3) | copy-start | bytes 786436
  91.4 11.7 %collective-permute-start.4 = (bf16[2048,2,32]{0,2,1:T(8,128)(2,1)S(1)}, bf16[2048,2,32]{0,2,1:T(8,128)(2,1)S(1)}, u32[]{:S(2)}, u32[]{:S(2)}) collective-permute-start(bf16[2048,2,32]{0,2,1:T(8,128)(2,1)S(1)} %collective-permute-done.3), channel_id=1, source_target_pairs={{0,1},{1,2},{2,3},{3,4},{4,5},{5,6},{6,7},{7,8},{8,9},{9,10},{10,1... | collective-permute-start | bytes 786440 | tf_op jit(solution)/shard_map/ppermute | solution.py:95
  103.1 170.6 %copy-start.10 = (bf16[2048,2,32]{0,2,1:T(8,128)(2,1)}, bf16[2048,2,32]{0,2,1:T(8,128)(2,1)S(1)}, u32[]{:S(2)}) copy-start(bf16[2048,2,32]{0,2,1:T(8,128)(2,1)S(1)} %collective-permute-done.4) | copy-start | bytes 786436
  103.1 15.1 %collective-permute-start.5 = (bf16[2048,2,32]{0,2,1:T(8,128)(2,1)S(1)}, bf16[2048,2,32]{0,2,1:T(8,128)(2,1)S(1)}, u32[]{:S(2)}, u32[]{:S(2)}) collective-permute-start(bf16[2048,2,32]{0,2,1:T(8,128)(2,1)S(1)} %collective-permute-done.4), channel_id=1, source_target_pairs={{0,1},{1,2},{2,3},{3,4},{4,5},{5,6},{6,7},{7,8},{8,9},{9,10},{10,1... | collective-permute-start | bytes 786440 | tf_op jit(solution)/shard_map/ppermute | solution.py:95
  118.9 11.6 %collective-permute-start.6 = (bf16[2048,2,32]{0,2,1:T(8,128)(2,1)S(1)}, bf16[2048,2,32]{0,2,1:T(8,128)(2,1)S(1)}, u32[]{:S(2)}, u32[]{:S(2)}) collective-permute-start(bf16[2048,2,32]{0,2,1:T(8,128)(2,1)S(1)} %collective-permute-done.5), channel_id=1, source_target_pairs={{0,1},{1,2},{2,3},{3,4},{4,5},{5,6},{6,7},{7,8},{8,9},{9,10},{10,1... | collective-permute-start | bytes 786440 | tf_op jit(solution)/shard_map/ppermute | solution.py:95
  131.2 17.8 %collective-permute-start.7 = (bf16[2048,2,32]{0,2,1:T(8,128)(2,1)S(1)}, bf16[2048,2,32]{0,2,1:T(8,128)(2,1)S(1)}, u32[]{:S(2)}, u32[]{:S(2)}) collective-permute-start(bf16[2048,2,32]{0,2,1:T(8,128)(2,1)S(1)} %collective-permute-done.6), channel_id=1, source_target_pairs={{0,1},{1,2},{2,3},{3,4},{4,5},{5,6},{6,7},{7,8},{8,9},{9,10},{10,1... | collective-permute-start | bytes 786440 | tf_op jit(solution)/shard_map/ppermute | solution.py:95
  149.6 17.5 %collective-permute-start.8 = (bf16[2048,2,32]{0,2,1:T(8,128)(2,1)S(1)}, bf16[2048,2,32]{0,2,1:T(8,128)(2,1)S(1)}, u32[]{:S(2)}, u32[]{:S(2)}) collective-permute-start(bf16[2048,2,32]{0,2,1:T(8,128)(2,1)S(1)} %collective-permute-done.7), channel_id=1, source_target_pairs={{0,1},{1,2},{2,3},{3,4},{4,5},{5,6},{6,7},{7,8},{8,9},{9,10},{10,1... | collective-permute-start | bytes 786440 | tf_op jit(solution)/shard_map/ppermute | solution.py:95
  167.8 17.2 %collective-permute-start.9 = (bf16[2048,2,32]{0,2,1:T(8,128)(2,1)S(1)}, bf16[2048,2,32]{0,2,1:T(8,128)(2,1)S(1)}, u32[]{:S(2)}, u32[]{:S(2)}) collective-permute-start(bf16[2048,2,32]{0,2,1:T(8,128)(2,1)S(1)} %collective-permute-done.8), channel_id=1, source_target_pairs={{0,1},{1,2},{2,3},{3,4},{4,5},{5,6},{6,7},{7,8},{8,9},{9,10},{10,1... | collective-permute-start | bytes 786440 | tf_op jit(solution)/shard_map/ppermute | solution.py:95
  185.8 11.6 %collective-permute-start.10 = (bf16[2048,2,32]{0,2,1:T(8,128)(2,1)S(1)}, bf16[2048,2,32]{0,2,1:T(8,128)(2,1)S(1)}, u32[]{:S(2)}, u32[]{:S(2)}) collective-permute-start(bf16[2048,2,32]{0,2,1:T(8,128)(2,1)S(1)} %collective-permute-done.9), channel_id=1, source_target_pairs={{0,1},{1,2},{2,3},{3,4},{4,5},{5,6},{6,7},{7,8},{8,9},{9,10},{10,1... | collective-permute-start | bytes 786440 | tf_op jit(solution)/shard_map/ppermute | solution.py:95
  198.0 12.7 %collective-permute-start.11 = (bf16[2048,2,32]{0,2,1:T(8,128)(2,1)S(1)}, bf16[2048,2,32]{0,2,1:T(8,128)(2,1)S(1)}, u32[]{:S(2)}, u32[]{:S(2)}) collective-permute-start(bf16[2048,2,32]{0,2,1:T(8,128)(2,1)S(1)} %collective-permute-done.10), channel_id=1, source_target_pairs={{0,1},{1,2},{2,3},{3,4},{4,5},{5,6},{6,7},{7,8},{8,9},{9,10},{10,1... | collective-permute-start | bytes 786440 | tf_op jit(solution)/shard_map/ppermute | solution.py:95
  211.4 13.9 %collective-permute-start.12 = (bf16[2048,2,32]{0,2,1:T(8,128)(2,1)S(1)}, bf16[2048,2,32]{0,2,1:T(8,128)(2,1)S(1)}, u32[]{:S(2)}, u32[]{:S(2)}) collective-permute-start(bf16[2048,2,32]{0,2,1:T(8,128)(2,1)S(1)} %collective-permute-done.11), channel_id=1, source_target_pairs={{0,1},{1,2},{2,3},{3,4},{4,5},{5,6},{6,7},{7,8},{8,9},{9,10},{10,1... | collective-permute-start | bytes 786440 | tf_op jit(solution)/shard_map/ppermute | solution.py:95
  226.0 13.5 %collective-permute-start.13 = (bf16[2048,2,32]{0,2,1:T(8,128)(2,1)S(1)}, bf16[2048,2,32]{0,2,1:T(8,128)(2,1)}, u32[]{:S(2)}, u32[]{:S(2)}) collective-permute-start(bf16[2048,2,32]{0,2,1:T(8,128)(2,1)S(1)} %collective-permute-done.12), channel_id=1, source_target_pairs={{0,1},{1,2},{2,3},{3,4},{4,5},{5,6},{6,7},{7,8},{8,9},{9,10},{10,1... | collective-permute-start | bytes 786440 | tf_op jit(solution)/shard_map/ppermute | solution.py:95
  239.4 78.4 %collective-permute-start.14 = (bf16[2048,2,32]{0,2,1:T(8,128)(2,1)}, bf16[2048,2,32]{0,2,1:T(8,128)(2,1)}, u32[]{:S(2)}, u32[]{:S(2)}) collective-permute-start(bf16[2048,2,32]{0,2,1:T(8,128)(2,1)} %collective-permute-done.13), channel_id=1, source_target_pairs={{0,1},{1,2},{2,3},{3,4},{4,5},{5,6},{6,7},{7,8},{8,9},{9,10},{10,1... | collective-permute-start | bytes 786440 | tf_op jit(solution)/shard_map/ppermute | solution.py:95
  502.6 5.7 collective-permute-start.15
  506.0 5.8 collective-permute-start.16
  519.3 76.2 %copy-start.20 = (f32[4,16,128]{2,1,0:T(8,128)S(1)}, f32[4,16,128]{2,1,0:T(8,128)}, u32[]{:S(2)}) copy-start(f32[4,16,128]{2,1,0:T(8,128)} %get-tuple-element.185) | copy-start | bytes 98308
  519.3 76.9 %copy-start.3 = (bf16[2048,1,128]{0,2,1:T(8,128)(2,1)S(1)}, bf16[2048,1,128]{0,2,1:T(8,128)(2,1)}, u32[]{:S(2)}) copy-start(bf16[2048,1,128]{0,2,1:T(8,128)(2,1)} %get-tuple-element.184) | copy-start | bytes 1572868
  666.9 5.5 collective-permute-start.17
  672.5 7.0 collective-permute-start.18
  (22 other events, 142.5 us)
Sparse Core Ops, SparseCore 0:
  9.5 69.3 all-gather.6
  81.9 103.6 all-gather.8
  548.9 71.9 all-gather.10
